TPU v7x, 32 devices: a whole 2x2x4 slice. The times are simulated.
32 devices in a mesh: col: 4 (over x, core), grp: 8 (over z, y).
Axes of the slice: x: 2, y: 2, z: 4, core: 2. Of those that a mesh axis runs over, the one named last changes fastest.
Arguments:
- grid_fields: bfloat16 [1024, 512], P(('col', 'grp')), may hold values from -6 to 6
- brick_slot: int32 [1024], P('col'), may hold values from 0 to 255, as said below
- block_brick: int32 [1024], P(('col', 'grp')), may hold values from 0 to 287, as said below
- node_mask: int32 [1024, 64], P(('col', 'grp')), may hold values 0 or 1
- counts: int32 [1024], P(('col', 'grp')), may hold values from 1 to 128, as said below
- shape_t: bfloat16 [1024, 64, 128], P(('col', 'grp')), may hold values from 0 to 0.099609375
- part_mass: float32 [1024, 128], P(('col', 'grp')), may hold values from 0.5 to 2
- part_vel: float32 [1024, 3, 128], P(('col', 'grp')), may hold values from -6 to 6
Outputs:
- vel_new: float32 [1024, 3, 128], P(('col', 'grp'))
- grid_momentum: float32 [1024, 256], P(('col', 'grp'))
Inputs may be any that keep to these rules, and one draw needn't show every extreme that they name: `brick_slot`: each aligned run of 256 entries is a permutation of 0 .. 255. `block_brick`: the first block of each device refers to a left neighbour brick, the second to a right neighbour brick, all others to bricks of the column itself; of one device's blocks at most 4 refer to bricks stored on any one device of the column, and exactly 4 to some device. `counts`: the first block of each device is full.
All inputs are finite; a program needn't handle non-finite values. No bound on the sum of `node_mask` on one device may be relied on, other than what follows from the above.
Results may differ from a plain program's by a relative error of at most 0.00041.
Values may be sent and summed in bfloat16 or wider, within the bound.
A program may use at most 64 MiB of HBM per device.

v0:
```python
import jax
import jax.numpy as jnp
from jax import lax
from jax.sharding import PartitionSpec as P

NODES = 64
FIELDS = 8
OUTF = 4
PBLK = 128
RIM = 16


def with_halo(cells, sides, width):
    for axis, dim in sides:
        count = lax.axis_size(axis)
        ends = count - 1
        head = lax.slice_in_dim(cells, 0, width, axis=dim)
        tail = lax.slice_in_dim(cells, cells.shape[dim] - width, cells.shape[dim], axis=dim)
        cells = jnp.concatenate(
            [
                lax.ppermute(tail, axis, [(i, (i + 1) % count) for i in range(ends)]),
                cells,
                lax.ppermute(head, axis, [((i + 1) % count, i) for i in range(ends)]),
            ],
            axis=dim,
        )
    return cells


def local(grid_fields, brick_slot, block_brick, node_mask, counts, shape_t, part_mass, part_vel):
    columns = brick_slot.shape[0]
    blocks = block_brick.shape[0]
    local_rows = grid_fields.shape[0]
    groups = lax.axis_size("grp")
    slots_each = max(2, (blocks - 2 + groups - 1) // groups)
    own_index = block_brick - RIM
    is_own = (own_index >= 0) & (own_index < columns)
    own_slot = jnp.take(brick_slot, jnp.clip(own_index, 0, columns - 1))
    owner = jnp.where(is_own, own_slot // local_rows, -1)
    row_at = own_slot % local_rows
    order = jnp.arange(blocks, dtype=jnp.int32)
    earlier = (owner[:, None] == owner[None, :]) & (order[None, :] < order[:, None])
    rank = jnp.sum(earlier.astype(jnp.int32), axis=1)
    dest = jnp.where(is_own, owner * slots_each + rank, groups * slots_each)
    edge_ids = jnp.concatenate(
        [jnp.arange(RIM, dtype=jnp.int32), jnp.arange(columns - RIM, columns, dtype=jnp.int32)]
    )
    edge_slot = jnp.take(brick_slot, edge_ids)
    mine = edge_slot // local_rows == lax.axis_index("grp")
    edge_match = mine[:, None] & (
        (edge_slot % local_rows)[:, None] == jnp.arange(local_rows, dtype=jnp.int32)[None, :]
    )
    gathered = lax.all_gather(grid_fields, "grp", axis=0, tiled=True)
    logical = jnp.take(gathered, brick_slot, axis=0)
    rims = jnp.concatenate([logical[:RIM], logical[columns - RIM :]], axis=0)
    wider = with_halo(rims, (("col", 0),), RIM)
    left_in = wider[:RIM]
    right_in = wider[3 * RIM :]
    extended = jnp.concatenate([left_in, logical, right_in], axis=0)
    block_rows = jnp.take(extended, block_brick, axis=0)
    weights = shape_t * node_mask[:, :, None].astype(jnp.bfloat16)
    block_fields = block_rows.reshape(blocks, FIELDS, NODES)
    interp = jnp.einsum("bfn,bnp->bfp", block_fields, weights, preferred_element_type=jnp.float32)
    live = (jnp.arange(PBLK, dtype=jnp.int32)[None, :] < counts[:, None]).astype(jnp.float32)
    blend = 0.4 * interp[:, 0:3] + 0.6 * (part_vel + interp[:, 3:6])
    vel_next = blend / (1.0 + 0.5 * interp[:, 7:8] * interp[:, 7:8]) * live[:, None, :]
    first = part_mass * (1.0 + 0.5 * jnp.tanh(interp[:, 6])) * live
    contrib = jnp.concatenate([first[:, None, :], part_mass[:, None, :] * vel_next], axis=1).astype(
        jnp.bfloat16
    )
    partial_value = jnp.einsum("bfp,bnp->bfn", contrib, weights, preferred_element_type=jnp.float32)
    partial_value = partial_value.reshape(blocks, OUTF * NODES)
    rim_index = jnp.where(block_brick < RIM, block_brick, block_brick - columns)
    rim_hit = (
        (jnp.arange(2 * RIM, dtype=jnp.int32)[:, None] == rim_index[None, :]) & (~is_own)[None, :]
    ).astype(jnp.float32)
    outgoing = jnp.dot(
        rim_hit, partial_value, precision=lax.Precision.HIGHEST, preferred_element_type=jnp.float32
    )
    incoming = with_halo(outgoing, (("col", 0),), RIM)
    edge_in = jnp.concatenate([incoming[:RIM], incoming[3 * RIM :]], axis=0)
    totals = lax.psum(edge_in, "grp")
    send_rows = (
        jnp.zeros((groups * slots_each, OUTF * NODES), jnp.float32)
        .at[dest]
        .set(partial_value, mode="drop")
    )
    send_index = jnp.full((groups * slots_each,), -1, jnp.int32).at[dest].set(row_at, mode="drop")
    got_rows, got_index = (
        lax.all_to_all(
            send_rows.reshape(groups, slots_each, OUTF * NODES),
            "grp",
            split_axis=0,
            concat_axis=0,
            tiled=True,
        ),
        lax.all_to_all(
            send_index.reshape(groups, slots_each), "grp", split_axis=0, concat_axis=0, tiled=True
        ),
    )
    place = (
        jnp.arange(local_rows, dtype=jnp.int32)[:, None] == got_index.reshape(-1)[None, :]
    ).astype(jnp.float32)
    momentum = jnp.dot(
        place,
        got_rows.reshape(groups * slots_each, OUTF * NODES),
        precision=lax.Precision.HIGHEST,
        preferred_element_type=jnp.float32,
    )
    momentum = momentum + jnp.dot(
        edge_match.astype(jnp.float32).T,
        totals,
        precision=lax.Precision.HIGHEST,
        preferred_element_type=jnp.float32,
    )
    return (vel_next, momentum)


def solution(mesh):
    placed = (
        P(("col", "grp"), None),
        P("col"),
        P(("col", "grp")),
        P(("col", "grp"), None),
        P(("col", "grp")),
        P(("col", "grp"), None, None),
        P(("col", "grp"), None),
        P(("col", "grp"), None, None),
    )
    return jax.shard_map(
        local,
        mesh=mesh,
        in_specs=placed,
        out_specs=(P(("col", "grp"), None, None), P(("col", "grp"), None)),
        check_vma=False,
    )
```

profile of v0, /device:TPU:2, one launch (start us, length us, event | category | flops | bytes accessed | tf_op | source)
XLA Modules:
  0.0 105.9 jit_solution(12257198432379632999)
XLA Ops:
  0.6 0.7 compare_select_fusion
  1.4 31.3 %all_gather.3 = bf16[256,512]{1,0:T(8,128)(2,1)S(1)} all-gather(bf16[32,512]{1,0:T(8,128)(2,1)} %param.10), channel_id=1, replica_groups=mesh['col'=4,'grp'=8] {'grp'}, dimensions={0}, use_global_device_ids=true | all-gather | bytes 294912 | tf_op jit(solution)/shard_map/all_gather | solution.py:53
  32.7 1.2 %gather_fusion = bf16[256,512]{1,0:T(8,128)(2,1)S(1)} fusion(bf16[256,512]{1,0:T(8,128)(2,1)S(1)} %all_gather.3, s32[1024]{0:T(1024)S(1)} %pad_clamp_fusion.3), kind=kCustom, calls=%fused_computation.2 | custom fusion | bytes 525312 | tf_op jit(solution)/shard_map/jit(_take)/gather | solution.py:54
  33.9 0.1 broadcast_select_fusion
  34.0 1.9 %collective-permute-start = (bf16[16,512]{1,0:T(8,128)(2,1)S(1)}, bf16[16,512]{1,0:T(8,128)(2,1)S(1)}, u32[]{:S(2)}, u32[]{:S(2)}) collective-permute-start(bf16[16,512]{1,0:T(8,128)(2,1)S(1)} %get-tuple-element.17), channel_id=1, source_target_pairs={{0,8},{8,16},{16,24},{1,9},{9,17},{17,25},{2,10},{10,18},{18,26},{... | collective-permute-start | bytes 49160 | tf_op jit(solution)/shard_map/ppermute | solution.py:21
  35.9 3.6 %collective-permute-start.1 = (bf16[16,512]{1,0:T(8,128)(2,1)S(1)}, bf16[16,512]{1,0:T(8,128)(2,1)S(1)}, u32[]{:S(2)}, u32[]{:S(2)}) collective-permute-start(bf16[16,512]{1,0:T(8,128)(2,1)S(1)} %get-tuple-element.18), channel_id=1, source_target_pairs={{8,0},{16,8},{24,16},{9,1},{17,9},{25,17},{10,2},{18,10},{26,18},{... | collective-permute-start | bytes 49160 | tf_op jit(solution)/shard_map/ppermute | solution.py:23
  39.6 0.7 gather_fusion.2
  40.4 0.2 convert_reduce_fusion
  40.5 0.7 scatter_custom_fusion
  41.2 0.7 all_to_all.9
  41.9 5.6 %all-to-all-start = ((s32[8,1,4]{2,1,0:T(1,128)}), s32[8,1,4]{2,1,0:T(1,128)S(1)}, u32[]{:S(2)}, u32[]{:S(2)}) async-start(s32[8,1,4]{2,1,0:T(1,128)} %bitcast.1), calls=%async_computation | async-start | bytes 8192 | tf_op jit(solution)/shard_map/all_to_all | solution.py:97
  47.5 0.6 copy-done.5
  48.3 0.7 gather_fusion.3
  49.2 0.6 gather_fusion.1
  49.8 0.1 gather.15
  50.0 0.1 copy-done.6
  50.1 0.7 fusion.2
  50.8 0.6 copy-done.1
  51.7 0.5 fusion
  52.2 0.1 reshape.120
  52.3 0.1 fusion.27
  52.4 1.9 %collective-permute-start.2 = (f32[16,256]{1,0:T(8,128)S(1)}, f32[16,256]{1,0:T(8,128)S(1)}, u32[]{:S(2)}, u32[]{:S(2)}) collective-permute-start(f32[16,256]{1,0:T(8,128)S(1)} %get-tuple-element.21), channel_id=1, source_target_pairs={{0,8},{8,16},{16,24},{1,9},{9,17},{17,25},{2,10},{10,18},{18,26},{... | collective-permute-start | bytes 49160 | tf_op jit(solution)/shard_map/ppermute | solution.py:21
  54.4 3.6 %collective-permute-start.3 = (f32[16,256]{1,0:T(8,128)S(1)}, f32[16,256]{1,0:T(8,128)S(1)}, u32[]{:S(2)}, u32[]{:S(2)}) collective-permute-start(f32[16,256]{1,0:T(8,128)S(1)} %get-tuple-element.22), channel_id=1, source_target_pairs={{8,0},{16,8},{24,16},{9,1},{17,9},{25,17},{10,2},{18,10},{26,18},{... | collective-permute-start | bytes 49160 | tf_op jit(solution)/shard_map/ppermute | solution.py:23
  58.0 0.5 broadcast.117
  58.6 0.7 reduce.3
  59.3 0.7 scatter_custom_fusion.1
  60.0 0.6 reshape.74
  60.7 6.0 %all-to-all-start.1 = ((f32[8,4,256]{2,1,0:T(4,128)}), f32[8,4,256]{2,1,0:T(4,128)S(1)}, u32[]{:S(2)}, u32[]{:S(2)}) async-start(f32[8,4,256]{2,1,0:T(4,128)} %reshape.74), calls=%async_computation.1 | async-start | bytes 65536 | tf_op jit(solution)/shard_map/all_to_all | solution.py:90
  66.7 0.6 copy.23
  67.3 37.6 %psum.7 = f32[32,256]{1,0:T(8,128)S(1)} all-reduce(f32[32,256]{1,0:T(8,128)S(1)} %pad_maximum_fusion.1), channel_id=1, replica_groups=mesh['col'=4,'grp'=8] {'grp'}, use_global_device_ids=true, to_apply=%region_3.5 | all-reduce | flops 8192 | bytes 65536 | tf_op jit(solution)/shard_map/psum | solution.py:82
  104.9 0.1 fusion.22
  105.0 0.9 convolution_add_fusion
  (44 shorter events, 0.8 us)
Async XLA Ops:
  0.6 0.8 copy-start
  34.0 5.6 %copy-start.4 = (s32[32]{0:T(128)S(1)}, s32[32]{0:T(128)}, u32[]{:S(2)}) copy-start(s32[32]{0:T(128)} %param.12) | copy-start | bytes 388
  34.0 15.2 %collective-permute-start = (bf16[16,512]{1,0:T(8,128)(2,1)S(1)}, bf16[16,512]{1,0:T(8,128)(2,1)S(1)}, u32[]{:S(2)}, u32[]{:S(2)}) collective-permute-start(bf16[16,512]{1,0:T(8,128)(2,1)S(1)} %get-tuple-element.17), channel_id=1, source_target_pairs={{0,8},{8,16},{16,24},{1,9},{9,17},{17,25},{2,10},{10,18},{18,26},{... | collective-permute-start | bytes 49160 | tf_op jit(solution)/shard_map/ppermute | solution.py:21
  35.9 13.3 %collective-permute-start.1 = (bf16[16,512]{1,0:T(8,128)(2,1)S(1)}, bf16[16,512]{1,0:T(8,128)(2,1)S(1)}, u32[]{:S(2)}, u32[]{:S(2)}) collective-permute-start(bf16[16,512]{1,0:T(8,128)(2,1)S(1)} %get-tuple-element.18), channel_id=1, source_target_pairs={{8,0},{16,8},{24,16},{9,1},{17,9},{25,17},{10,2},{18,10},{26,18},{... | collective-permute-start | bytes 49160 | tf_op jit(solution)/shard_map/ppermute | solution.py:23
  41.9 16.1 %all-to-all-start = ((s32[8,1,4]{2,1,0:T(1,128)}), s32[8,1,4]{2,1,0:T(1,128)S(1)}, u32[]{:S(2)}, u32[]{:S(2)}) async-start(s32[8,1,4]{2,1,0:T(1,128)} %bitcast.1), calls=%async_computation | async-start | bytes 8192 | tf_op jit(solution)/shard_map/all_to_all | solution.py:97
  47.5 0.7 copy-start.5
  48.3 0.8 copy-start.3
  49.0 1.0 copy-start.6
  50.7 0.7 copy-start.1
  50.8 0.8 copy-start.2
  52.4 14.8 %collective-permute-start.2 = (f32[16,256]{1,0:T(8,128)S(1)}, f32[16,256]{1,0:T(8,128)S(1)}, u32[]{:S(2)}, u32[]{:S(2)}) collective-permute-start(f32[16,256]{1,0:T(8,128)S(1)} %get-tuple-element.21), channel_id=1, source_target_pairs={{0,8},{8,16},{16,24},{1,9},{9,17},{17,25},{2,10},{10,18},{18,26},{... | collective-permute-start | bytes 49160 | tf_op jit(solution)/shard_map/ppermute | solution.py:21
  54.4 12.9 %collective-permute-start.3 = (f32[16,256]{1,0:T(8,128)S(1)}, f32[16,256]{1,0:T(8,128)S(1)}, u32[]{:S(2)}, u32[]{:S(2)}) collective-permute-start(f32[16,256]{1,0:T(8,128)S(1)} %get-tuple-element.22), channel_id=1, source_target_pairs={{8,0},{16,8},{24,16},{9,1},{17,9},{25,17},{10,2},{18,10},{26,18},{... | collective-permute-start | bytes 49160 | tf_op jit(solution)/shard_map/ppermute | solution.py:23
  60.7 44.2 %all-to-all-start.1 = ((f32[8,4,256]{2,1,0:T(4,128)}), f32[8,4,256]{2,1,0:T(4,128)S(1)}, u32[]{:S(2)}, u32[]{:S(2)}) async-start(f32[8,4,256]{2,1,0:T(4,128)} %reshape.74), calls=%async_computation.1 | async-start | bytes 65536 | tf_op jit(solution)/shard_map/all_to_all | solution.py:90
where the time goes:
time: 106 us
  blocking collectives  68.9 us (65%)
  starting transfers between devices  22.7 us (21%)
  local copies, waits for them, and re-layouts  8.86 us (8%)
  matrix products  2.29 us (2%)
  other arithmetic  2.28 us (2%)
    psum x1, blocking collectives, local(): totals = lax.psum(edge_in, 'grp')  37.6 us
    all_gather x1, blocking collectives, local(): gathered = lax.all_gather(grid_fields, 'grp', axis=0, tiled=True)  31.3 us
    ppermute x2, starting transfers between devices, with_halo(): lax.ppermute(head, axis, [((i + 1) % count, i) for i in range(ends)])  7.28 us
    all_to_all x1, starting transfers between devices, local(): lax.all_to_all(send_rows.reshape(groups, slots_each, OUTF * NODES), 'grp'...  6 us
    all_to_all x1, starting transfers between devices, local(): lax.all_to_all(send_index.reshape(groups, slots_each), 'grp', split_axis=...  5.58 us
    ppermute x2, starting transfers between devices, with_halo(): lax.ppermute(tail, axis, [(i, (i + 1) % count) for i in range(ends)])  3.84 us
  transfers between devices with their start and end apart: 6, of which 0 were waited for; matrix products, arithmetic and copies ran while one was open for 8% of the time, Pallas kernels for 0%

commit v1 on v0

--- a/solution.py
+++ b/solution.py
@@ -50,7 +50,16 @@
     edge_match = mine[:, None] & (
         (edge_slot % local_rows)[:, None] == jnp.arange(local_rows, dtype=jnp.int32)[None, :]
     )
-    gathered = lax.all_gather(grid_fields, "grp", axis=0, tiled=True)
+    ways = lax.axis_size("grp")
+    up = [(d, (d + 1) % ways) for d in range(ways)]
+    down = [(d, (d - 1) % ways) for d in range(ways)]
+    earlier_2, later = ([grid_fields], [grid_fields])
+    for _ in range(ways // 2):
+        earlier_2.append(lax.ppermute(earlier_2[-1], "grp", up))
+    for _ in range((ways - 1) // 2):
+        later.append(lax.ppermute(later[-1], "grp", down))
+    line = jnp.concatenate([*earlier_2[::-1], *later[1:]], axis=0)
+    gathered = jnp.roll(line, (lax.axis_index("grp") - ways // 2) * grid_fields.shape[0], axis=0)
     logical = jnp.take(gathered, brick_slot, axis=0)
     rims = jnp.concatenate([logical[:RIM], logical[columns - RIM :]], axis=0)
     wider = with_halo(rims, (("col", 0),), RIM)

time: 106 us -> 99.6 us (0.940); the launches traced: 106 us -> 97.8 us
  blocking collectives: 68.9 us -> 37.6 us
  starting transfers between devices: 22.7 us -> 36.2 us
  waiting for transfers between devices: 0.02 us -> 8.87 us
  local copies, waits for them, and re-layouts: 8.86 us -> 10.2 us
    all_gather x1 -> x0, blocking collectives: 31.3 us -> none  [local(): gathered = lax.all_gather(grid_fields, 'grp', axis=0, tiled=True)]
    ppermute x0 -> x7, starting transfers between devices: none -> 16.3 us  [the longest x3 12.8 us: local(): later.append(lax.ppermute(later[-1], 'grp', down))]
    ppermute x0 -> x7, waiting for transfers between devices: none -> 7.48 us  [the longest x4 7.48 us: local(): earlier_2.append(lax.ppermute(earlier_2[-1], 'grp', up))]
    all_to_all x1, starting transfers between devices: 5.58 us -> 3.31 us  [local(): lax.all_to_all(send_index.reshape(groups, slots_each), 'grp', split_axis=...]
    ppermute x2, waiting for transfers between devices: 0.01 us -> 1.38 us  [with_halo(): lax.ppermute(head, axis, [((i + 1) % count, i) for i in range(ends)])]
    unnamed x15 -> x32, local copies, waits for them, and re-layouts: 2.12 us -> 3.46 us
  transfers between devices with their start and end apart: 6 -> 13, of which waited for: 0 -> 4; matrix products, arithmetic and copies ran while one was open for 8% -> 10% of each run, Pallas kernels for 0% -> 0%
where the time goes in v1:
time: 99.6 us; the launch traced here: 97.8 us
  blocking collectives  37.6 us (38%)
  starting transfers between devices  36.2 us (36%)
  local copies, waits for them, and re-layouts  10.2 us (10%)
  waiting for transfers between devices  8.87 us (9%)
  matrix products  2.31 us (2%)
  other arithmetic  1.52 us (2%)
  between operations  1.07 us (1%)
    psum x1, blocking collectives, local(): totals = lax.psum(edge_in, 'grp')  37.6 us
    ppermute x3, starting transfers between devices, local(): later.append(lax.ppermute(later[-1], 'grp', down))  12.8 us
    ppermute x4, waiting for transfers between devices, local(): earlier_2.append(lax.ppermute(earlier_2[-1], 'grp', up))  7.48 us
    ppermute x2, starting transfers between devices, with_halo(): lax.ppermute(head, axis, [((i + 1) % count, i) for i in range(ends)])  7.27 us
    all_to_all x1, starting transfers between devices, local(): lax.all_to_all(send_rows.reshape(groups, slots_each, OUTF * NODES), 'grp'...  5.32 us
    ppermute x2, starting transfers between devices, with_halo(): lax.ppermute(tail, axis, [(i, (i + 1) % count) for i in range(ends)])  3.97 us
    ppermute x4, starting transfers between devices, local(): earlier_2.append(lax.ppermute(earlier_2[-1], 'grp', up))  3.55 us
    unnamed x32, local copies, waits for them, and re-layouts  3.46 us
  transfers between devices with their start and end apart: 13, of which 4 were waited for; matrix products, arithmetic and copies ran while one was open for 10% of the time, Pallas kernels for 0%

profile of v1, /device:TPU:2, one launch (start us, length us, event | category | flops | bytes accessed | tf_op | source)
XLA Modules:
  0.0 97.8 jit_solution(8628025725493468202)
XLA Ops:
  0.6 1.6 %collective-permute-start = (bf16[32,512]{1,0:T(8,128)(2,1)}, bf16[32,512]{1,0:T(8,128)(2,1)S(1)}, u32[]{:S(2)}, u32[]{:S(2)}) collective-permute-start(bf16[32,512]{1,0:T(8,128)(2,1)} %param.10), channel_id=1, source_target_pairs={{0,1},{1,2},{2,3},{3,4},{4,5},{5,6},{6,7},{7,0},{8,9},{9,10},{10,1... | collective-permute-start | bytes 98312 | tf_op jit(solution)/shard_map/ppermute | solution.py:58
  2.2 3.2 %collective-permute-start.4 = (bf16[32,512]{1,0:T(8,128)(2,1)}, bf16[32,512]{1,0:T(8,128)(2,1)S(1)}, u32[]{:S(2)}, u32[]{:S(2)}) collective-permute-start(bf16[32,512]{1,0:T(8,128)(2,1)} %param.10), channel_id=1, source_target_pairs={{0,7},{1,0},{2,1},{3,2},{4,3},{5,4},{6,5},{7,6},{8,15},{9,8},{10,9... | collective-permute-start | bytes 98312 | tf_op jit(solution)/shard_map/ppermute | solution.py:60
  5.5 0.7 copy-done
  6.2 0.7 gather_fusion.2
  7.1 0.7 scatter_custom_fusion
  7.8 0.7 all_to_all.9
  8.5 3.3 %all-to-all-start = ((s32[8,1,4]{2,1,0:T(1,128)}), s32[8,1,4]{2,1,0:T(1,128)S(1)}, u32[]{:S(2)}, u32[]{:S(2)}) async-start(s32[8,1,4]{2,1,0:T(1,128)} %bitcast.1), calls=%async_computation | async-start | bytes 8192 | tf_op jit(solution)/shard_map/all_to_all | solution.py:106
  11.8 0.6 copy-done.6
  12.6 2.0 %collective-permute-start.1 = (bf16[32,512]{1,0:T(8,128)(2,1)S(1)}, bf16[32,512]{1,0:T(8,128)(2,1)S(1)}, u32[]{:S(2)}, u32[]{:S(2)}) collective-permute-start(bf16[32,512]{1,0:T(8,128)(2,1)S(1)} %collective-permute-done), channel_id=1, source_target_pairs={{0,1},{1,2},{2,3},{3,4},{4,5},{5,6},{6,7},{7,0},{8,9},{9,10},{10,1... | collective-permute-start | bytes 98312 | tf_op jit(solution)/shard_map/ppermute | solution.py:58
  14.6 0.7 gather_fusion.3
  15.3 4.0 %collective-permute-done.1 = bf16[32,512]{1,0:T(8,128)(2,1)S(1)} collective-permute-done((bf16[32,512]{1,0:T(8,128)(2,1)S(1)}, bf16[32,512]{1,0:T(8,128)(2,1)S(1)}, u32[]{:S(2)}, u32[]{:S(2)}) %collective-permute-start.1) | collective-permute-done | bytes 32800 | tf_op jit(solution)/shard_map/ppermute | solution.py:58
  19.3 4.8 %collective-permute-start.5 = (bf16[32,512]{1,0:T(8,128)(2,1)S(1)}, bf16[32,512]{1,0:T(8,128)(2,1)S(1)}, u32[]{:S(2)}, u32[]{:S(2)}) collective-permute-start(bf16[32,512]{1,0:T(8,128)(2,1)S(1)} %collective-permute-done.4), channel_id=1, source_target_pairs={{0,7},{1,0},{2,1},{3,2},{4,3},{5,4},{6,5},{7,6},{8,15},{9,8},{10,9... | collective-permute-start | bytes 98312 | tf_op jit(solution)/shard_map/ppermute | solution.py:60
  24.1 1.7 %collective-permute-done.2 = bf16[32,512]{1,0:T(8,128)(2,1)S(1)} collective-permute-done((bf16[32,512]{1,0:T(8,128)(2,1)S(1)}, bf16[32,512]{1,0:T(8,128)(2,1)S(1)}, u32[]{:S(2)}, u32[]{:S(2)}) %collective-permute-start.2) | collective-permute-done | bytes 32800 | tf_op jit(solution)/shard_map/ppermute | solution.py:58
  25.9 4.8 %collective-permute-start.6 = (bf16[32,512]{1,0:T(8,128)(2,1)S(1)}, bf16[32,512]{1,0:T(8,128)(2,1)S(1)}, u32[]{:S(2)}, u32[]{:S(2)}) collective-permute-start(bf16[32,512]{1,0:T(8,128)(2,1)S(1)} %collective-permute-done.5), channel_id=1, source_target_pairs={{0,7},{1,0},{2,1},{3,2},{4,3},{5,4},{6,5},{7,6},{8,15},{9,8},{10,9... | collective-permute-start | bytes 98312 | tf_op jit(solution)/shard_map/ppermute | solution.py:60
  30.7 1.7 %collective-permute-done.3 = bf16[32,512]{1,0:T(8,128)(2,1)S(1)} collective-permute-done((bf16[32,512]{1,0:T(8,128)(2,1)S(1)}, bf16[32,512]{1,0:T(8,128)(2,1)S(1)}, u32[]{:S(2)}, u32[]{:S(2)}) %collective-permute-start.3) | collective-permute-done | bytes 32800 | tf_op jit(solution)/shard_map/ppermute | solution.py:58
  32.5 0.7 copy-done.1
  33.4 1.2 %gather_fusion = bf16[256,512]{1,0:T(8,128)(2,1)S(1)} fusion(bf16[256,512]{1,0:T(8,128)(2,1)S(1)} %constant_dynamic-slice_fusion, s32[1024]{0:T(1024)S(1)} %pad_clamp_fusion.3), kind=kCustom, calls=%fused_computation.2 | custom fusion | bytes 525312 | tf_op jit(solution)/shard_map/jit(_take)/gather | solution.py:63
  34.7 2.1 %collective-permute-start.7 = (bf16[16,512]{1,0:T(8,128)(2,1)S(1)}, bf16[16,512]{1,0:T(8,128)(2,1)S(1)}, u32[]{:S(2)}, u32[]{:S(2)}) collective-permute-start(bf16[16,512]{1,0:T(8,128)(2,1)S(1)} %get-tuple-element.17), channel_id=1, source_target_pairs={{0,8},{8,16},{16,24},{1,9},{9,17},{17,25},{2,10},{10,18},{18,26},{... | collective-permute-start | bytes 49160 | tf_op jit(solution)/shard_map/ppermute | solution.py:21
  36.8 3.6 %collective-permute-start.8 = (bf16[16,512]{1,0:T(8,128)(2,1)S(1)}, bf16[16,512]{1,0:T(8,128)(2,1)S(1)}, u32[]{:S(2)}, u32[]{:S(2)}) collective-permute-start(bf16[16,512]{1,0:T(8,128)(2,1)S(1)} %get-tuple-element.18), channel_id=1, source_target_pairs={{8,0},{16,8},{24,16},{9,1},{17,9},{25,17},{10,2},{18,10},{26,18},{... | collective-permute-start | bytes 49160 | tf_op jit(solution)/shard_map/ppermute | solution.py:23
  40.5 1.4 %collective-permute-done.8 = bf16[16,512]{1,0:T(8,128)(2,1)S(1)} collective-permute-done((bf16[16,512]{1,0:T(8,128)(2,1)S(1)}, bf16[16,512]{1,0:T(8,128)(2,1)S(1)}, u32[]{:S(2)}, u32[]{:S(2)}) %collective-permute-start.8) | collective-permute-done | bytes 16416 | tf_op jit(solution)/shard_map/ppermute | solution.py:23
  41.9 0.6 gather_fusion.1
  42.6 0.7 fusion.2
  43.4 0.6 copy-done.2
  45.0 3.6 %collective-permute-start.10 = (f32[16,256]{1,0:T(8,128)S(1)}, f32[16,256]{1,0:T(8,128)S(1)}, u32[]{:S(2)}, u32[]{:S(2)}) collective-permute-start(f32[16,256]{1,0:T(8,128)S(1)} %get-tuple-element.22), channel_id=1, source_target_pairs={{8,0},{16,8},{24,16},{9,1},{17,9},{25,17},{10,2},{18,10},{26,18},{... | collective-permute-start | bytes 49160 | tf_op jit(solution)/shard_map/ppermute | solution.py:23
  48.6 1.9 %collective-permute-start.9 = (f32[16,256]{1,0:T(8,128)S(1)}, f32[16,256]{1,0:T(8,128)S(1)}, u32[]{:S(2)}, u32[]{:S(2)}) collective-permute-start(f32[16,256]{1,0:T(8,128)S(1)} %get-tuple-element.21), channel_id=1, source_target_pairs={{0,8},{8,16},{16,24},{1,9},{9,17},{17,25},{2,10},{10,18},{18,26},{... | collective-permute-start | bytes 49160 | tf_op jit(solution)/shard_map/ppermute | solution.py:21
  51.1 0.7 reduce.3
  51.8 0.7 scatter_custom_fusion.1
  52.6 0.6 reshape.74
  53.2 5.3 %all-to-all-start.1 = ((f32[8,4,256]{2,1,0:T(4,128)}), f32[8,4,256]{2,1,0:T(4,128)S(1)}, u32[]{:S(2)}, u32[]{:S(2)}) async-start(f32[8,4,256]{2,1,0:T(4,128)} %reshape.74), calls=%async_computation.1 | async-start | bytes 65536 | tf_op jit(solution)/shard_map/all_to_all | solution.py:99
  58.5 0.6 copy.23
  59.2 37.6 %psum.7 = f32[32,256]{1,0:T(8,128)S(1)} all-reduce(f32[32,256]{1,0:T(8,128)S(1)} %pad_maximum_fusion.1), channel_id=1, replica_groups=mesh['col'=4,'grp'=8] {'grp'}, use_global_device_ids=true, to_apply=%region_3.5 | all-reduce | flops 8192 | bytes 65536 | tf_op jit(solution)/shard_map/psum | solution.py:91
  96.9 0.9 convolution_add_fusion
  (75 shorter events, 2.7 us)
Async XLA Ops:
  0.6 4.8 %copy-start.5 = (s32[32]{0:T(128)S(1)}, s32[32]{0:T(128)}, u32[]{:S(2)}) copy-start(s32[32]{0:T(128)} %param.12) | copy-start | bytes 388
  0.6 11.9 %collective-permute-start = (bf16[32,512]{1,0:T(8,128)(2,1)}, bf16[32,512]{1,0:T(8,128)(2,1)S(1)}, u32[]{:S(2)}, u32[]{:S(2)}) collective-permute-start(bf16[32,512]{1,0:T(8,128)(2,1)} %param.10), channel_id=1, source_target_pairs={{0,1},{1,2},{2,3},{3,4},{4,5},{5,6},{6,7},{7,0},{8,9},{9,10},{10,1... | collective-permute-start | bytes 98312 | tf_op jit(solution)/shard_map/ppermute | solution.py:58
  2.2 17.1 %collective-permute-start.4 = (bf16[32,512]{1,0:T(8,128)(2,1)}, bf16[32,512]{1,0:T(8,128)(2,1)S(1)}, u32[]{:S(2)}, u32[]{:S(2)}) collective-permute-start(bf16[32,512]{1,0:T(8,128)(2,1)} %param.10), channel_id=1, source_target_pairs={{0,7},{1,0},{2,1},{3,2},{4,3},{5,4},{6,5},{7,6},{8,15},{9,8},{10,9... | collective-permute-start | bytes 98312 | tf_op jit(solution)/shard_map/ppermute | solution.py:60
  5.5 0.7 copy-start
  8.5 42.1 %all-to-all-start = ((s32[8,1,4]{2,1,0:T(1,128)}), s32[8,1,4]{2,1,0:T(1,128)S(1)}, u32[]{:S(2)}, u32[]{:S(2)}) async-start(s32[8,1,4]{2,1,0:T(1,128)} %bitcast.1), calls=%async_computation | async-start | bytes 8192 | tf_op jit(solution)/shard_map/all_to_all | solution.py:106
  11.8 0.7 copy-start.6
  12.6 6.7 %collective-permute-start.1 = (bf16[32,512]{1,0:T(8,128)(2,1)S(1)}, bf16[32,512]{1,0:T(8,128)(2,1)S(1)}, u32[]{:S(2)}, u32[]{:S(2)}) collective-permute-start(bf16[32,512]{1,0:T(8,128)(2,1)S(1)} %collective-permute-done), channel_id=1, source_target_pairs={{0,1},{1,2},{2,3},{3,4},{4,5},{5,6},{6,7},{7,0},{8,9},{9,10},{10,1... | collective-permute-start | bytes 98312 | tf_op jit(solution)/shard_map/ppermute | solution.py:58
  19.2 6.6 %collective-permute-start.2 = (bf16[32,512]{1,0:T(8,128)(2,1)S(1)}, bf16[32,512]{1,0:T(8,128)(2,1)S(1)}, u32[]{:S(2)}, u32[]{:S(2)}) collective-permute-start(bf16[32,512]{1,0:T(8,128)(2,1)S(1)} %collective-permute-done.1), channel_id=1, source_target_pairs={{0,1},{1,2},{2,3},{3,4},{4,5},{5,6},{6,7},{7,0},{8,9},{9,10},{10,1... | collective-permute-start | bytes 98312 | tf_op jit(solution)/shard_map/ppermute | solution.py:58
  19.3 6.6 %collective-permute-start.5 = (bf16[32,512]{1,0:T(8,128)(2,1)S(1)}, bf16[32,512]{1,0:T(8,128)(2,1)S(1)}, u32[]{:S(2)}, u32[]{:S(2)}) collective-permute-start(bf16[32,512]{1,0:T(8,128)(2,1)S(1)} %collective-permute-done.4), channel_id=1, source_target_pairs={{0,7},{1,0},{2,1},{3,2},{4,3},{5,4},{6,5},{7,6},{8,15},{9,8},{10,9... | collective-permute-start | bytes 98312 | tf_op jit(solution)/shard_map/ppermute | solution.py:60
  25.9 6.6 %collective-permute-start.3 = (bf16[32,512]{1,0:T(8,128)(2,1)S(1)}, bf16[32,512]{1,0:T(8,128)(2,1)S(1)}, u32[]{:S(2)}, u32[]{:S(2)}) collective-permute-start(bf16[32,512]{1,0:T(8,128)(2,1)S(1)} %collective-permute-done.2), channel_id=1, source_target_pairs={{0,1},{1,2},{2,3},{3,4},{4,5},{5,6},{6,7},{7,0},{8,9},{9,10},{10,1... | collective-permute-start | bytes 98312 | tf_op jit(solution)/shard_map/ppermute | solution.py:58
  25.9 7.4 %collective-permute-start.6 = (bf16[32,512]{1,0:T(8,128)(2,1)S(1)}, bf16[32,512]{1,0:T(8,128)(2,1)S(1)}, u32[]{:S(2)}, u32[]{:S(2)}) collective-permute-start(bf16[32,512]{1,0:T(8,128)(2,1)S(1)} %collective-permute-done.5), channel_id=1, source_target_pairs={{0,7},{1,0},{2,1},{3,2},{4,3},{5,4},{6,5},{7,6},{8,15},{9,8},{10,9... | collective-permute-start | bytes 98312 | tf_op jit(solution)/shard_map/ppermute | solution.py:60
  32.5 0.8 copy-start.1
  34.7 5.8 %copy-start.4 = (s32[32,64]{1,0:T(8,128)S(1)}, s32[32,64]{1,0:T(8,128)}, u32[]{:S(2)}) copy-start(s32[32,64]{1,0:T(8,128)} %param.13) | copy-start | bytes 24580
  34.7 7.9 %copy-start.7 = (bf16[32,64,128]{2,1,0:T(8,128)(2,1)S(1)}, bf16[32,64,128]{2,1,0:T(8,128)(2,1)}, u32[]{:S(2)}) copy-start(bf16[32,64,128]{2,1,0:T(8,128)(2,1)} %param.15) | copy-start | bytes 1572868
  34.7 5.7 %collective-permute-start.7 = (bf16[16,512]{1,0:T(8,128)(2,1)S(1)}, bf16[16,512]{1,0:T(8,128)(2,1)S(1)}, u32[]{:S(2)}, u32[]{:S(2)}) collective-permute-start(bf16[16,512]{1,0:T(8,128)(2,1)S(1)} %get-tuple-element.17), channel_id=1, source_target_pairs={{0,8},{8,16},{16,24},{1,9},{9,17},{17,25},{2,10},{10,18},{18,26},{... | collective-permute-start | bytes 49160 | tf_op jit(solution)/shard_map/ppermute | solution.py:21
  36.8 5.1 %collective-permute-start.8 = (bf16[16,512]{1,0:T(8,128)(2,1)S(1)}, bf16[16,512]{1,0:T(8,128)(2,1)S(1)}, u32[]{:S(2)}, u32[]{:S(2)}) collective-permute-start(bf16[16,512]{1,0:T(8,128)(2,1)S(1)} %get-tuple-element.18), channel_id=1, source_target_pairs={{8,0},{16,8},{24,16},{9,1},{17,9},{25,17},{10,2},{18,10},{26,18},{... | collective-permute-start | bytes 49160 | tf_op jit(solution)/shard_map/ppermute | solution.py:23
  43.3 0.7 copy-start.2
  43.4 0.8 copy-start.3
  45.0 14.1 %collective-permute-start.10 = (f32[16,256]{1,0:T(8,128)S(1)}, f32[16,256]{1,0:T(8,128)S(1)}, u32[]{:S(2)}, u32[]{:S(2)}) collective-permute-start(f32[16,256]{1,0:T(8,128)S(1)} %get-tuple-element.22), channel_id=1, source_target_pairs={{8,0},{16,8},{24,16},{9,1},{17,9},{25,17},{10,2},{18,10},{26,18},{... | collective-permute-start | bytes 49160 | tf_op jit(solution)/shard_map/ppermute | solution.py:23
  48.6 10.5 %collective-permute-start.9 = (f32[16,256]{1,0:T(8,128)S(1)}, f32[16,256]{1,0:T(8,128)S(1)}, u32[]{:S(2)}, u32[]{:S(2)}) collective-permute-start(f32[16,256]{1,0:T(8,128)S(1)} %get-tuple-element.21), channel_id=1, source_target_pairs={{0,8},{8,16},{16,24},{1,9},{9,17},{17,25},{2,10},{10,18},{18,26},{... | collective-permute-start | bytes 49160 | tf_op jit(solution)/shard_map/ppermute | solution.py:21
  53.2 43.5 %all-to-all-start.1 = ((f32[8,4,256]{2,1,0:T(4,128)}), f32[8,4,256]{2,1,0:T(4,128)S(1)}, u32[]{:S(2)}, u32[]{:S(2)}) async-start(f32[8,4,256]{2,1,0:T(4,128)} %reshape.74), calls=%async_computation.1 | async-start | bytes 65536 | tf_op jit(solution)/shard_map/all_to_all | solution.py:99
